TPU v7x, 32 devices: a whole 2x2x4 slice. The times are simulated.
32 devices in a mesh: dp: 2 (over x), row: 4 (over z), col: 4 (over y, core).
Axes of the slice: x: 2, y: 2, z: 4, core: 2. Of those that a mesh axis runs over, the one named last changes fastest.
Arguments:
- inputs: bfloat16 [2304, 4, 384], P(('dp', 'col'), 'row'), may hold values from -6 to 6
- cotangent: bfloat16 [2304, 4, 384], P(('dp', 'col'), 'row'), may hold values from -6 to 6
- slot_mask: int32 [8], replicated, may hold values from 0 to 1, as said below
- region_ids: int32 [24, 24], replicated, may hold values from 0 to 8, as said below
- offset_index: int32 [144, 144], replicated, may hold values from 0 to 528, as said below
- first_gain: float32 [768], P('row'), may hold values from 0.5 to 1.5
- first_shift: float32 [768], P('row'), may hold values from -1.75 to 1.75
- query_key_value: bfloat16 [384, 3, 4, 384], P('row', None, 'col'), may hold values from -0.21875 to 0.21875
- query_value_bias: float32 [2, 768], P(None, 'col'), may hold values from -3 to 3
- position_table: float32 [529, 24], P(None, 'col'), may hold values from -6 to 6
- output_weight: bfloat16 [384, 4, 384], P('col', 'row'), may hold values from -0.625 to 0.625
- output_bias: float32 [768], P('row'), may hold values from -1.75 to 1.75
- second_gain: float32 [768], P('row'), may hold values from 0.5 to 1.5
- second_shift: float32 [768], P('row'), may hold values from -1.75 to 1.75
- expand_weight: bfloat16 [768, 3072], P('row', 'col'), may hold values from -0.21875 to 0.21875
- expand_bias: float32 [3072], P('col'), may hold values from -1.75 to 1.75
- contract_weight: bfloat16 [1536, 4, 384], P('col', 'row'), may hold values from -0.109375 to 0.109375
- contract_bias: float32 [768], P('row'), may hold values from -1.75 to 1.75
Outputs:
- layer_output: bfloat16 [2304, 4, 384], P(('dp', 'col'), 'row')
- input_gradient: float32 [2304, 4, 384], P(('dp', 'col'), 'row')
- first_gain_gradient: float32 [768], P('row')
- first_shift_gradient: float32 [768], P('row')
- query_key_value_gradient: float32 [384, 3, 4, 384], P('row', None, 'col')
- query_value_bias_gradient: float32 [2, 768], P(None, 'col')
- position_table_gradient: float32 [529, 24], P(None, 'col')
- output_weight_gradient: float32 [384, 4, 384], P('col', 'row')
- output_bias_gradient: float32 [768], P('row')
- second_gain_gradient: float32 [768], P('row')
- second_shift_gradient: float32 [768], P('row')
- expand_weight_gradient: float32 [768, 3072], P('row', 'col')
- expand_bias_gradient: float32 [3072], P('col')
- contract_weight_gradient: float32 [1536, 4, 384], P('col', 'row')
- contract_bias_gradient: float32 [768], P('row')
Inputs may be any that keep to these rules, and one draw needn't show every extreme that they name: `slot_mask`: 1 on the first slots and 0 on the rest; at least one slot of each kind. `region_ids`: 3 times a band of the token's row plus a band of its column; bands 0, 1, 2 cut at two drawn places along each side, each band non-empty. `offset_index`: a one-to-one relabelling of the offset between two window positions: equal offsets give equal entries, and every entry appears.
All inputs are finite; a program needn't handle non-finite values.
Results may differ from a plain program's by a relative error of at most 0.012.
Values may be sent and summed in bfloat16 or wider, within the bound.
No kernel may reach another device: no remote copies, remote signals or barrier semaphores. Data moves between devices by JAX's collectives and lax.ppermute only.
A program may use at most 128 MiB of HBM per device.

v0:
```python
import jax
import jax.numpy as jnp
from jax import lax
from jax.sharding import PartitionSpec as P

HEAD_DIM = 32
SIDE = 24
WIN = 12
SHIFT = 6
REL = 529
NORM_EPS = 1e-05
MASK_FILL = -100.0
SPLIT_DIMS = (((1,), (1,)), ((), ()))
ROW_DIMS = (((0,), (0,)), ((), ()))


def unpair_local(paired):
    return paired.reshape(paired.shape[0] * 2, paired.shape[2] // 2)


def pair_local(matrix):
    return matrix.reshape(matrix.shape[0] // 2, 1, matrix.shape[1] * 2)


def unpair_joined(paired):
    halves = paired.shape[0]
    single = paired.shape[3] // 2
    return paired.reshape(halves, 3, 2, single).transpose(0, 2, 1, 3).reshape(halves * 2, 3, single)


def pair_joined(joined):
    count = joined.shape[0]
    single = joined.shape[2]
    return (
        joined.reshape(count // 2, 2, 3, single)
        .transpose(0, 2, 1, 3)
        .reshape(count // 2, 3, 1, 2 * single)
    )


def to_windows(source, head_count):
    images = source.shape[0] // (SIDE * SIDE)
    blocks = SIDE // WIN
    shaped = source.reshape(images, SIDE, SIDE, head_count, HEAD_DIM)
    shaped = jnp.roll(shaped, (-SHIFT, -SHIFT), axis=(1, 2))
    shaped = shaped.reshape(images, blocks, WIN, blocks, WIN, head_count, HEAD_DIM)
    shaped = shaped.transpose(0, 1, 3, 5, 2, 4, 6)
    return shaped.reshape(images * blocks * blocks, head_count, WIN * WIN, HEAD_DIM)


def from_windows(windowed, head_count):
    blocks = SIDE // WIN
    images = windowed.shape[0] // (blocks * blocks)
    shaped = windowed.reshape(images, blocks, blocks, head_count, WIN, WIN, HEAD_DIM)
    shaped = shaped.transpose(0, 1, 4, 2, 5, 3, 6).reshape(images, SIDE, SIDE, head_count, HEAD_DIM)
    shaped = jnp.roll(shaped, (SHIFT, SHIFT), axis=(1, 2))
    return shaped.reshape(images * SIDE * SIDE, head_count * HEAD_DIM)


def region_mask(region_ids):
    blocks = SIDE // WIN
    labels = (
        region_ids.reshape(blocks, WIN, blocks, WIN)
        .transpose(0, 2, 1, 3)
        .reshape(blocks * blocks, WIN * WIN)
    )
    return jnp.where(labels[:, :, None] == labels[:, None, :], 0.0, MASK_FILL).astype(jnp.float32)


def norm_totals(first_term, second_term):
    return lax.psum((jnp.sum(first_term, -1), jnp.sum(second_term, -1)), "row")


def norm_forward(values, norm_gain, norm_shift, width):
    totals, squares = norm_totals(values, values * values)
    centre = totals / width
    spread = squares / width - centre * centre
    inverse = lax.rsqrt(spread + NORM_EPS)
    normed = (values - centre[:, None]) * inverse[:, None]
    return (normed, inverse, normed * norm_gain + norm_shift)


def norm_backward(upstream, normed, inverse, norm_gain, width):
    scaled = upstream * norm_gain
    totals, crossed = norm_totals(scaled, scaled * normed)
    return inverse[:, None] * (
        scaled - totals[:, None] / width - normed * (crossed[:, None] / width)
    )


def norm_spread(values):
    return lax.all_gather(values, "col", axis=0, tiled=True)


def head_collect(values):
    return lax.all_gather(values, "row", axis=0, tiled=True)


def cotangent_spread(values):
    return lax.all_gather(values, "col", axis=0, tiled=True)


def gradient_collect(values):
    return lax.all_gather(values, "row", axis=0, tiled=True)


def width_sums(gathered, weight, row_count):

    def partial_rows(begin_at, how_many):
        return jnp.dot(gathered, weight, preferred_element_type=jnp.float32)

    return lax.psum_scatter(
        partial_rows(jnp.int32(0), lax.axis_size("row") * row_count),
        "row",
        scatter_dimension=0,
        tiled=True,
    )


def token_sums(gathered, weight, row_count):

    def partial_rows(begin_at, how_many):
        return jnp.dot(gathered, weight, preferred_element_type=jnp.float32)

    return lax.psum_scatter(
        partial_rows(jnp.int32(0), lax.axis_size("col") * row_count),
        "col",
        scatter_dimension=0,
        tiled=True,
    )


def width_back(gathered, weight, row_count):

    def partial_rows(begin_at, how_many):
        return lax.dot_general(gathered, weight, SPLIT_DIMS, preferred_element_type=jnp.float32)

    return lax.psum_scatter(
        partial_rows(jnp.int32(0), lax.axis_size("row") * row_count),
        "row",
        scatter_dimension=0,
        tiled=True,
    )


def token_back(gathered, weight, row_count):

    def partial_rows(begin_at, how_many):
        return lax.dot_general(gathered, weight, SPLIT_DIMS, preferred_element_type=jnp.float32)

    return lax.psum_scatter(
        partial_rows(jnp.int32(0), lax.axis_size("col") * row_count),
        "col",
        scatter_dimension=0,
        tiled=True,
    )


def exact_gelu(values):
    return jax.nn.gelu(values, approximate=False)


def gelu_backward(pre_values, upstream):
    return jax.vjp(exact_gelu, pre_values)[1](upstream)[0]


def window_scores(queries, keys_in, bias_block, mask_block):
    products = jnp.einsum("nhid,nhjd->nhij", queries, keys_in, preferred_element_type=jnp.float32)
    return products + bias_block[None] + mask_block[:, None]


def local(
    inputs,
    cotangent,
    slot_mask,
    region_ids,
    offset_index,
    first_gain,
    first_shift,
    query_key_value,
    query_value_bias,
    position_table,
    output_weight,
    output_bias,
    second_gain,
    second_shift,
    expand_weight,
    expand_bias,
    contract_weight,
    contract_bias,
):
    inputs_rows = unpair_local(inputs)
    cotangent_rows = unpair_local(cotangent)
    joined_plain = unpair_joined(query_key_value)
    output_plain = unpair_local(output_weight)
    contract_plain = unpair_local(contract_weight)
    row_size = lax.axis_size("row")
    local_tokens = inputs_rows.shape[0]
    image_tokens = SIDE * SIDE
    width = inputs_rows.shape[1] * row_size
    head_width = joined_plain.shape[2]
    head_local = head_width // HEAD_DIM
    scale = float(HEAD_DIM) ** (-0.5)
    joined_weight = joined_plain.reshape(joined_plain.shape[0], 3 * head_width)
    mask_block = region_mask(region_ids)
    bias_block = jnp.take(position_table, offset_index, axis=0).transpose(2, 0, 1)
    residual = inputs_rows.astype(jnp.float32)
    normed_one, inverse_one, scaled_one = norm_forward(residual, first_gain, first_shift, width)
    spread_one = norm_spread(scaled_one.astype(jnp.bfloat16))
    projected = width_sums(spread_one, joined_weight, image_tokens).reshape(
        image_tokens, 3, head_width
    )
    queries = to_windows(
        ((projected[:, 0] + query_value_bias[0]) * scale).astype(jnp.bfloat16), head_local
    )
    keys_win = to_windows(projected[:, 1].astype(jnp.bfloat16), head_local)
    values_win = to_windows(
        (projected[:, 2] + query_value_bias[1]).astype(jnp.bfloat16), head_local
    )
    scores = window_scores(queries, keys_win, bias_block, mask_block)
    largest = jnp.max(scores, -1, keepdims=True)
    powers = jnp.exp(scores - largest)
    summed = jnp.sum(powers, -1, keepdims=True)
    log_total = largest + jnp.log(summed)
    attended = jnp.einsum(
        "nhij,nhjd->nhid",
        (powers / summed).astype(jnp.bfloat16),
        values_win,
        preferred_element_type=jnp.float32,
    )
    attended_all = head_collect(from_windows(attended.astype(jnp.bfloat16), head_local))
    residual_mid = residual + token_sums(attended_all, output_plain, local_tokens) + output_bias
    normed_two, inverse_two, scaled_two = norm_forward(
        residual_mid, second_gain, second_shift, width
    )
    spread_two = norm_spread(scaled_two.astype(jnp.bfloat16))
    pre_values = width_sums(spread_two, expand_weight, image_tokens) + expand_bias
    hidden_all = head_collect(exact_gelu(pre_values).astype(jnp.bfloat16))
    layer_output = (
        residual_mid + token_sums(hidden_all, contract_plain, local_tokens) + contract_bias
    ).astype(jnp.bfloat16)
    flags = lax.dynamic_slice_in_dim(slot_mask, lax.axis_index("dp") * row_size, row_size)
    positions = lax.axis_index("col") * local_tokens + jnp.arange(local_tokens, dtype=jnp.int32)
    image_slot = positions // image_tokens
    token_flag = jnp.sum(
        jnp.where(
            image_slot[:, None] == jnp.arange(row_size, dtype=jnp.int32)[None, :], flags[None, :], 0
        ),
        axis=1,
    ).astype(jnp.float32)
    upstream = cotangent_rows.astype(jnp.float32) * token_flag[:, None]
    upstream_all = cotangent_spread(upstream.astype(jnp.bfloat16))
    contract_grad = lax.dot_general(
        hidden_all, upstream_all, ROW_DIMS, preferred_element_type=jnp.float32
    )
    contract_bias_grad = jnp.sum(upstream_all, 0, dtype=jnp.float32)
    hidden_grad = width_back(upstream_all, contract_plain, image_tokens)
    pre_grad_all = gradient_collect(gelu_backward(pre_values, hidden_grad).astype(jnp.bfloat16))
    expand_grad = lax.dot_general(
        spread_two, pre_grad_all, ROW_DIMS, preferred_element_type=jnp.float32
    )
    expand_bias_grad = jnp.sum(pre_grad_all, 0, dtype=jnp.float32)
    normed_grad_two = token_back(pre_grad_all, expand_weight, local_tokens)
    second_gain_grad = jnp.sum(normed_grad_two * normed_two, 0)
    second_shift_grad = jnp.sum(normed_grad_two, 0)
    residual_grad = upstream + norm_backward(
        normed_grad_two, normed_two, inverse_two, second_gain, width
    )
    residual_all = cotangent_spread(residual_grad.astype(jnp.bfloat16))
    output_grad = lax.dot_general(
        attended_all, residual_all, ROW_DIMS, preferred_element_type=jnp.float32
    )
    output_bias_grad = jnp.sum(residual_all, 0, dtype=jnp.float32)
    attended_grad = to_windows(
        width_back(residual_all, output_plain, image_tokens).astype(jnp.bfloat16), head_local
    )
    probs = jnp.exp(window_scores(queries, keys_win, bias_block, mask_block) - log_total)
    value_grad = jnp.einsum(
        "nhij,nhid->nhjd",
        probs.astype(jnp.bfloat16),
        attended_grad,
        preferred_element_type=jnp.float32,
    )
    prob_grad = jnp.einsum(
        "nhid,nhjd->nhij", attended_grad, values_win, preferred_element_type=jnp.float32
    )
    score_grad = (probs * (prob_grad - jnp.sum(probs * prob_grad, -1, keepdims=True))).astype(
        jnp.bfloat16
    )
    query_grad = jnp.einsum(
        "nhij,nhjd->nhid", score_grad, keys_win, preferred_element_type=jnp.float32
    )
    key_grad = jnp.einsum(
        "nhij,nhid->nhjd", score_grad, queries, preferred_element_type=jnp.float32
    )
    bias_grad = jnp.sum(score_grad, 0, dtype=jnp.float32)
    table_grad = jax.ops.segment_sum(
        bias_grad.transpose(1, 2, 0).reshape(-1, head_local),
        offset_index.reshape(-1),
        num_segments=REL,
    )
    joined_grad = jnp.stack(
        [
            from_windows((query_grad * scale).astype(jnp.bfloat16), head_local),
            from_windows(key_grad.astype(jnp.bfloat16), head_local),
            from_windows(value_grad.astype(jnp.bfloat16), head_local),
        ],
        axis=1,
    ).reshape(image_tokens, 3 * head_width)
    joined_all = gradient_collect(joined_grad)
    joined_weight_grad = lax.dot_general(
        spread_one, joined_all, ROW_DIMS, preferred_element_type=jnp.float32
    ).reshape(-1, 3, head_width)
    column_totals = jnp.sum(joined_all, 0, dtype=jnp.float32).reshape(3, head_width)
    query_value_grad = jnp.stack([column_totals[0], column_totals[2]])
    normed_grad_one = token_back(joined_all, joined_weight, local_tokens)
    first_gain_grad = jnp.sum(normed_grad_one * normed_one, 0)
    first_shift_grad = jnp.sum(normed_grad_one, 0)
    input_gradient = residual_grad + norm_backward(
        normed_grad_one, normed_one, inverse_one, first_gain, width
    )
    summed_weights = lax.psum(
        (
            pair_joined(joined_weight_grad),
            query_value_grad,
            pair_local(output_grad),
            output_bias_grad,
            expand_grad,
            expand_bias_grad,
            pair_local(contract_grad),
            contract_bias_grad,
        ),
        "dp",
    )
    summed_norms = lax.psum(
        (first_gain_grad, first_shift_grad, second_gain_grad, second_shift_grad), ("dp", "col")
    )
    summed_table = lax.psum(table_grad, ("dp", "row"))
    return (
        pair_local(layer_output),
        pair_local(input_gradient),
        summed_norms[0],
        summed_norms[1],
        summed_weights[0],
        summed_weights[1],
        summed_table,
        summed_weights[2],
        summed_weights[3],
        summed_norms[2],
        summed_norms[3],
        summed_weights[4],
        summed_weights[5],
        summed_weights[6],
        summed_weights[7],
    )


def solution(mesh):
    in_specs = (
        P(("dp", "col"), "row", None),
        P(("dp", "col"), "row", None),
        P(),
        P(),
        P(),
        P("row"),
        P("row"),
        P("row", None, "col", None),
        P(None, "col"),
        P(None, "col"),
        P("col", "row", None),
        P("row"),
        P("row"),
        P("row"),
        P("row", "col"),
        P("col"),
        P("col", "row", None),
        P("row"),
    )
    out_specs = (
        P(("dp", "col"), "row", None),
        P(("dp", "col"), "row", None),
        P("row"),
        P("row"),
        P("row", None, "col", None),
        P(None, "col"),
        P(None, "col"),
        P("col", "row", None),
        P("row"),
        P("row"),
        P("row"),
        P("row", "col"),
        P("col"),
        P("col", "row", None),
        P("row"),
    )
    return jax.shard_map(local, mesh=mesh, in_specs=in_specs, out_specs=out_specs, check_vma=False)
```

profile of v0, /device:TPU:0, one launch (start us, length us, event | category | flops | bytes accessed | tf_op | source)
XLA Modules:
  0.0 1180.4 jit_solution(9655379731013944303)
XLA Ops:
  9.7 13.7 %all-reduce.4 = (f32[576]{0:T(1024)S(1)}, f32[576]{0:T(1024)S(1)}) all-reduce(f32[576]{0:T(1024)S(1)} %get-tuple-element.101, f32[576]{0:T(1024)S(1)} %get-tuple-element.100), channel_id=1, replica_groups=mesh['dp'=2,'row'=4,'col'=4] {'row'}, use_global_device_ids=true, to_apply=%region_3.4 | all-reduce | flops 1152 | bytes 9216 | tf_op jit(solution)/shard_map/psum | solution.py:71
  23.8 9.7 all-gather
  41.0 39.4 %gather_fusion = f32[20736,6]{1,0:T(8,128)} fusion(f32[529,6]{1,0:T(8,128)S(1)} %copy.285, s32[21504]{0:T(1024)S(1)} %pad_clamp_fusion), kind=kCustom, calls=%fused_computation | custom fusion | bytes 1078272 | tf_op jit(solution)/shard_map/jit(_take)/gather | solution.py:206
  80.4 11.6 copy.286
  94.1 46.5 %reduce-scatter.19.cloned.1.call-done = f32[576,576]{1,0:T(8,128)} async-done(((f32[2304,576]{1,0:T(8,128)}), f32[576,576]{1,0:T(8,128)}) %reduce-scatter.19.cloned.1.call-update) | async-done | bytes 1327120 | tf_op jit(solution)/shard_map/reduce_scatter | solution.py:112
  212.2 21.2 %all-gather.1 = bf16[4,576,192]{1,2,0:T(8,128)(2,1)S(1)} all-gather(bf16[1,576,192]{1,2,0:T(8,128)(2,1)S(1)} %reshape.291), channel_id=1, replica_groups=mesh['dp'=2,'row'=4,'col'=4] {'row'}, dimensions={0}, use_global_device_ids=true | all-gather | bytes 1105920 | tf_op jit(solution)/shard_map/all_gather | solution.py:96
  241.9 9.9 all-gather.3
  255.6 4.1 fusion.41
  259.7 13.0 %reduce-scatter.25.cloned.1.call-done = f32[576,192]{1,0:T(8,128)} async-done(((f32[2304,192]{1,0:T(8,128)}), f32[576,192]{1,0:T(8,128)}) %reduce-scatter.25.cloned.1.call-update) | async-done | bytes 442384 | tf_op jit(solution)/shard_map/reduce_scatter | solution.py:125
  274.0 12.0 %all-reduce.3 = (f32[576]{0:T(1024)S(1)}, f32[576]{0:T(1024)S(1)}) all-reduce(f32[576]{0:T(1024)S(1)} %get-tuple-element.99, f32[576]{0:T(1024)S(1)} %get-tuple-element.98), channel_id=1, replica_groups=mesh['dp'=2,'row'=4,'col'=4] {'row'}, use_global_device_ids=true, to_apply=%region_11.12 | all-reduce | flops 1152 | bytes 9216 | tf_op jit(solution)/shard_map/psum | solution.py:71
  287.2 8.7 all-gather.2
  299.7 4.1 fusion.39
  304.2 94.6 %reduce-scatter.23.cloned.1.call-done = f32[576,768]{1,0:T(8,128)} async-done(((f32[2304,768]{1,0:T(8,128)}), f32[576,768]{1,0:T(8,128)}) %reduce-scatter.23.cloned.1.call-update) | async-done | bytes 1769488 | tf_op jit(solution)/shard_map/reduce_scatter | solution.py:138
  398.8 126.1 %reduce-scatter.21.cloned.1.call-done = f32[576,768]{1,0:T(8,128)} async-done(((f32[2304,768]{1,0:T(8,128)}), f32[576,768]{1,0:T(8,128)}) %reduce-scatter.21.cloned.1.call-update) | async-done | bytes 1769488 | tf_op jit(solution)/shard_map/reduce_scatter | solution.py:112
  525.0 6.8 add_convert_fusion.1
  535.1 67.4 %all-gather.11.cloned.1.call-done = bf16[2304,768]{1,0:T(8,128)(2,1)} async-done(((bf16[576,768]{1,0:T(8,128)(2,1)}), bf16[2304,768]{1,0:T(8,128)(2,1)}) %all-gather.11.cloned.1.call-update) | async-done | bytes 3538960 | tf_op jit(solution)/shard_map/all_gather | solution.py:104
  602.5 4.6 fusion.42
  607.1 65.5 %all-gather.9.cloned.1.call-done = bf16[2304,768]{1,0:T(8,128)(2,1)} async-done(((bf16[576,768]{1,0:T(8,128)(2,1)}), bf16[2304,768]{1,0:T(8,128)(2,1)}) %all-gather.9.cloned.1.call-update) | async-done | bytes 3538960 | tf_op jit(solution)/shard_map/all_gather | solution.py:96
  672.6 4.5 fusion.40
  677.1 29.8 %reduce-scatter.29.cloned.1.call-done = f32[576,192]{1,0:T(8,128)} async-done(((f32[2304,192]{1,0:T(8,128)}), f32[576,192]{1,0:T(8,128)}) %reduce-scatter.29.cloned.1.call-update) | async-done | bytes 442384 | tf_op jit(solution)/shard_map/reduce_scatter | solution.py:151
  709.0 11.8 %all-reduce.2 = (f32[576]{0:T(1024)S(1)}, f32[576]{0:T(1024)S(1)}) all-reduce(f32[576]{0:T(1024)S(1)} %get-tuple-element.91, f32[576]{0:T(1024)S(1)} %get-tuple-element.95), channel_id=1, replica_groups=mesh['dp'=2,'row'=4,'col'=4] {'row'}, use_global_device_ids=true, to_apply=%region_20.21 | all-reduce | flops 1152 | bytes 9216 | tf_op jit(solution)/shard_map/psum | solution.py:71
  721.5 21.1 %reduce-scatter.27.cloned.1.call-done = f32[576,192]{1,0:T(8,128)} async-done(((f32[2304,192]{1,0:T(8,128)}), f32[576,192]{1,0:T(8,128)}) %reduce-scatter.27.cloned.1.call-update) | async-done | bytes 442384 | tf_op jit(solution)/shard_map/reduce_scatter | solution.py:125
  745.4 9.3 all-gather.4
  761.3 47.8 %reduce-scatter.31.cloned.1.call-done = f32[576,192]{1,0:T(8,128)} async-done(((f32[2304,192]{1,0:T(8,128)}), f32[576,192]{1,0:T(8,128)}) %reduce-scatter.31.cloned.1.call-update) | async-done | bytes 442384
  896.1 4.3 fusion.46
  901.7 48.1 %all-gather.13.cloned.1.call-done = bf16[2304,576]{1,0:T(8,128)(2,1)} async-done(((bf16[576,576]{1,0:T(8,128)(2,1)}), bf16[2304,576]{1,0:T(8,128)(2,1)}) %all-gather.13.cloned.1.call-update) | async-done | bytes 2654224 | tf_op jit(solution)/shard_map/all_gather | solution.py:104
  969.0 11.2 copy.342
  980.2 113.1 %scatter_custom_fusion = f32[529,6]{1,0:T(8,128)} fusion(s32[20736]{0:T(1024)} %reshape.280, f32[20736,6]{1,0:T(8,128)} %bitcast.156, f32[]{:T(128)} %constant.48.clone.1), kind=kCustom, calls=%fused_computation.94 | custom fusion | flops 124416 | bytes 13208 | tf_op jit(solution)/shard_map/scatter-add | solution.py:297
  1093.3 40.7 %psum.159 = f32[529,6]{1,0:T(8,128)S(1)} all-reduce(f32[529,6]{1,0:T(8,128)} %scatter_custom_fusion), channel_id=1, replica_groups=mesh['dp'=2,'row'=4,'col'=4] {'dp','row'}, use_global_device_ids=true, to_apply=%region_37.38 | all-reduce | flops 3174 | bytes 25392 | tf_op jit(solution)/shard_map/psum | solution.py:338
  1135.4 5.7 all-reduce.5
  1147.4 9.2 all-reduce.1
  1159.4 12.4 %all-reduce = (f32[192]{0:T(256)}, f32[192]{0:T(256)}, f32[192]{0:T(256)}, f32[192]{0:T(256)}) all-reduce(f32[192]{0:T(256)S(1)} %get-tuple-element.92, f32[192]{0:T(256)S(1)} %get-tuple-element.97, f32[192]{0:T(256)S(1)} %copy-done.51, f32[192]{0:T(256)S(1)} %copy-done.52), channel_id=1, replica_groups=mesh['dp'=2,'row'=4,'col'=4] {'dp','col'}, use_global_device_ids=true, to_apply=%region_29.30 | all-reduce | flops 768 | bytes 6144 | tf_op jit(solution)/shard_map/psum | solution.py:335
  (311 shorter events, 237.1 us)
Async XLA Ops:
  7.2 292.5 %copy-start = (bf16[192,768]{1,0:T(8,128)(2,1)S(1)}, bf16[192,768]{1,0:T(8,128)(2,1)}, u32[]{:S(2)}) copy-start(bf16[192,768]{1,0:T(8,128)(2,1)} %param.32) | copy-start | bytes 884740
  7.2 16.2 %copy-start.47 = (f32[192]{0:T(256)S(1)}, f32[192]{0:T(256)}, u32[]{:S(2)}) copy-start(f32[192]{0:T(256)} %param.23) | copy-start | bytes 2308
  7.2 16.2 %copy-start.54 = (f32[192]{0:T(256)S(1)}, f32[192]{0:T(256)}, u32[]{:S(2)}) copy-start(f32[192]{0:T(256)} %param.24) | copy-start | bytes 2308
  7.2 133.3 %reduce-scatter.19.cloned.1.call-start = ((), (), s32[]{:S(2)}) async-start(), calls=%async_computation.8 | async-start | bytes 7372800 | tf_op jit(solution)/shard_map/reduce_scatter | solution.py:112
  9.3 25.8 %copy-start.24 = (bf16[192,576]{1,0:T(8,128)(2,1)}, bf16[192,576]{1,0:T(8,128)(2,1)S(1)}, u32[]{:S(2)}) copy-start(bf16[192,576]{1,0:T(8,128)(2,1)S(1)} %reshape_reshape.6) | copy-start | bytes 663556
  9.4 263.3 %copy-start.4 = (f32[576,192]{1,0:T(8,128)}, f32[576,192]{1,0:T(8,128)S(1)}, u32[]{:S(2)}) copy-start(f32[576,192]{1,0:T(8,128)S(1)} %reshape.268) | copy-start | bytes 1327108
  38.7 234.0 %reduce-scatter.25.cloned.1.call-start = ((), (), s32[]{:S(2)}) async-start(), calls=%async_computation.14 | async-start | bytes 2949120 | tf_op jit(solution)/shard_map/reduce_scatter | solution.py:125
  239.3 159.5 %reduce-scatter.23.cloned.1.call-start = ((), (), s32[]{:S(2)}) async-start(), calls=%async_computation.11 | async-start | bytes 8847360 | tf_op jit(solution)/shard_map/reduce_scatter | solution.py:138
  240.1 11.7 copy-start.43
  241.3 14.2 %copy-start.17 = (bf16[768,192]{1,0:T(8,128)(2,1)}, bf16[768,192]{1,0:T(8,128)(2,1)S(1)}, u32[]{:S(2)}) copy-start(bf16[768,192]{1,0:T(8,128)(2,1)S(1)} %reshape.251) | copy-start | bytes 884740
  255.6 634.4 %copy-start.9 = (bf16[2304,192]{0,1:T(8,128)(2,1)}, bf16[2304,192]{0,1:T(8,128)(2,1)S(1)}, u32[]{:S(2)}) copy-start(bf16[2304,192]{0,1:T(8,128)(2,1)S(1)} %reshape.296) | copy-start | bytes 2654212
  259.6 13.0 %copy-start.55 = (f32[192]{0:T(256)S(1)}, f32[192]{0:T(256)}, u32[]{:S(2)}) copy-start(f32[192]{0:T(256)} %param.29) | copy-start | bytes 2308
  259.7 26.4 %copy-start.49 = (f32[192]{0:T(256)S(1)}, f32[192]{0:T(256)}, u32[]{:S(2)}) copy-start(f32[192]{0:T(256)} %param.30) | copy-start | bytes 2308
  259.7 265.3 %reduce-scatter.21.cloned.1.call-start = ((), (), s32[]{:S(2)}) async-start(), calls=%async_computation.9 | async-start | bytes 8847360 | tf_op jit(solution)/shard_map/reduce_scatter | solution.py:112
  303.7 221.2 %copy-start.45 = (f32[768]{0:T(1024)S(1)}, f32[768]{0:T(1024)}, u32[]{:S(2)}) copy-start(f32[768]{0:T(1024)} %param.33) | copy-start | bytes 9220
  303.8 298.7 %all-gather.11.cloned.1.call-start = ((), (), s32[]{:S(2)}) async-start(), calls=%async_computation.12 | async-start | bytes 4423680 | tf_op jit(solution)/shard_map/all_gather | solution.py:104
  531.8 140.8 %all-gather.9.cloned.1.call-start = ((), (), s32[]{:S(2)}) async-start(), calls=%async_computation.10 | async-start | bytes 4423680 | tf_op jit(solution)/shard_map/all_gather | solution.py:96
  535.0 171.9 %reduce-scatter.29.cloned.1.call-start = ((), (), s32[]{:S(2)}) async-start(), calls=%async_computation.16 | async-start | bytes 2949120 | tf_op jit(solution)/shard_map/reduce_scatter | solution.py:151
  607.0 65.5 %copy-start.18 = (bf16[768,192]{1,0:T(8,128)(2,1)S(1)}, bf16[768,192]{1,0:T(8,128)(2,1)}, u32[]{:S(2)}) copy-start(bf16[768,192]{1,0:T(8,128)(2,1)} %copy-done.17) | copy-start | bytes 884740
  607.1 135.5 %reduce-scatter.27.cloned.1.call-start = ((), (), s32[]{:S(2)}) async-start(), calls=%async_computation.15 | async-start | bytes 2949120 | tf_op jit(solution)/shard_map/reduce_scatter | solution.py:125
  677.1 29.9 %copy-start.50 = (f32[192]{0:T(256)S(1)}, f32[192]{0:T(256)}, u32[]{:S(2)}) copy-start(f32[192]{0:T(256)} %param.30) | copy-start | bytes 2308
  677.1 65.5 %copy-start.14 = (f32[576,192]{1,0:T(8,128)S(1)}, f32[576,192]{1,0:T(8,128)}, u32[]{:S(2)}) copy-start(f32[576,192]{1,0:T(8,128)} %copy-done.13) | copy-start | bytes 1327108
  677.1 132.1 %reduce-scatter.31.cloned.1.call-start = ((), (), s32[]{:S(2)}) async-start(), calls=%async_computation.17 | async-start | bytes 2949120
  758.4 141.9 %copy-start.6 = (bf16[2304,192]{0,1:T(8,128)(2,1)}, bf16[2304,192]{0,1:T(8,128)(2,1)S(1)}, u32[]{:S(2)}) copy-start(bf16[2304,192]{0,1:T(8,128)(2,1)S(1)} %reshape.298) | copy-start | bytes 2654212
  760.6 189.2 %all-gather.13.cloned.1.call-start = ((), (), s32[]{:S(2)}) async-start(), calls=%async_computation.13 | async-start | bytes 3686400 | tf_op jit(solution)/shard_map/all_gather | solution.py:104
  889.9 251.2 %all-reduce.9.cloned.1.call-start = ((), (), s32[]{:S(2)}) async-start(), calls=%async_computation.19 | async-start | bytes 3538944 | tf_op jit(solution)/shard_map/psum | solution.py:322
  958.4 187.4 %reduce-scatter.33.cloned.1.call-start = ((), (), s32[]{:S(2)}) async-start(), calls=%async_computation.18 | async-start | bytes 2949120 | tf_op jit(solution)/shard_map/reduce_scatter | solution.py:151
  1135.3 21.3 %copy-start.23 = (f32[576,192]{1,0:T(8,128)S(1)}, f32[576,192]{1,0:T(8,128)}, u32[]{:S(2)}) copy-start(f32[576,192]{1,0:T(8,128)} %get-tuple-element.127) | copy-start | bytes 1327108
  1147.3 12.1 %copy-start.51 = (f32[192]{0:T(256)S(1)}, f32[192]{0:T(256)}, u32[]{:S(2)}) copy-start(f32[192]{0:T(256)} %get-tuple-element.90) | copy-start | bytes 2308
  1147.3 12.1 %copy-start.52 = (f32[192]{0:T(256)S(1)}, f32[192]{0:T(256)}, u32[]{:S(2)}) copy-start(f32[192]{0:T(256)} %get-tuple-element.96) | copy-start | bytes 2308
  1147.4 24.4 %copy-start.39 = (f32[96,1,384]{2,1,0:T(1,128)S(1)}, f32[96,1,384]{2,1,0:T(1,128)}, u32[]{:S(2)}) copy-start(f32[96,1,384]{2,1,0:T(1,128)} %get-tuple-element.153) | copy-start | bytes 442372
  1156.6 15.9 %copy-start.34 = (f32[192,768]{1,0:T(8,128)S(1)}, f32[192,768]{1,0:T(8,128)}, u32[]{:S(2)}) copy-start(f32[192,768]{1,0:T(8,128)} %get-tuple-element.157) | copy-start | bytes 1769476
  (43 other events, 120.9 us)
Sparse Core Ops, SparseCore 0:
  38.8 101.6 reduce-scatter.18
  239.4 33.2 reduce-scatter.24
  275.1 123.6 reduce-scatter.22
  401.1 123.8 reduce-scatter.20
  531.9 70.4 all-gather.10
  604.0 68.5 all-gather.8
  675.3 31.6 reduce-scatter.28
  709.5 33.0 reduce-scatter.26
  760.7 48.4 reduce-scatter.30
  890.0 59.7 all-gather.12
  958.5 54.9 all-reduce.8
  1015.9 33.0 reduce-scatter.32
where the time goes:
time: 1190 us; the launch traced here: 1180 us
  waiting for transfers between devices  560 us (47%)
  local copies, waits for them, and re-layouts  217 us (18%)
  other arithmetic  172 us (14%)
  blocking collectives  164 us (14%)
  matrix products  50.2 us (4%)
  between operations  15.4 us (1%)
    reduce_scatter x2, waiting for transfers between devices, width_sums(): lax.psum_scatter(partial_rows(jnp.int32(0), lax.axis_size('row') * row_co...  173 us
    all_gather x2, waiting for transfers between devices, gradient_collect(): return lax.all_gather(values, 'row', axis=0, tiled=True)  115 us
    scatter-add x1, other arithmetic, local(): jax.ops.segment_sum(bias_grad.transpose(1, 2, 0).reshape(-1, head_local),...  113 us
    reduce_scatter x1, waiting for transfers between devices, width_back(): lax.psum_scatter(partial_rows(jnp.int32(0), lax.axis_size('row') * row_co...  94.6 us
    all_gather x1, waiting for transfers between devices, head_collect(): return lax.all_gather(values, 'row', axis=0, tiled=True)  65.5 us
    gather x2, local copies, waits for them, and re-layouts, local(): jnp.take(position_table, offset_index, axis=0).transpose(2, 0, 1)  51.1 us
    unnamed x13, waiting for transfers between devices  48 us
    psum x4, blocking collectives, norm_totals(): return lax.psum((jnp.sum(first_term, -1), jnp.sum(second_term, -1)), 'row')  46.8 us
  transfers between devices with their start and end apart: 12, of which 10 were waited for; matrix products, arithmetic and copies ran while one was open for 20% of the time, Pallas kernels for 0%

commit v1 on v0

--- a/solution.py
+++ b/solution.py
@@ -14,6 +14,18 @@
 ROW_DIMS = (((0,), (0,)), ((), ()))
 
 
+def gather_by_bits(x, axis, dim):
+    ways, here, hop = (lax.axis_size(axis), lax.axis_index(axis), x.shape[dim])
+    line, have = (x, 1)
+    while have < ways:
+        line = jnp.concatenate(
+            [line, lax.ppermute(line, axis, [(d, (d - have) % ways) for d in range(ways)])],
+            axis=dim,
+        )
+        have = 2 * have
+    return jnp.roll(line, here * hop, axis=dim)
+
+
 def unpair_local(paired):
     return paired.reshape(paired.shape[0] * 2, paired.shape[2] // 2)
 
@@ -93,7 +105,7 @@
 
 
 def head_collect(values):
-    return lax.all_gather(values, "row", axis=0, tiled=True)
+    return gather_by_bits(values, "row", 0)
 
 
 def cotangent_spread(values):

time: 1190 us -> 1200 us (level)
  blocking collectives: 164 us -> 142 us
  waiting for transfers between devices: 560 us -> 577 us
    ppermute x0 -> x4, waiting for transfers between devices: none -> 101 us  [gather_by_bits(): lax.ppermute(line, axis, [(d, (d - have) % ways) for d in range(ways)])]
    all_gather x1 -> x0, waiting for transfers between devices: 65.5 us -> none  [head_collect(): return lax.all_gather(values, 'row', axis=0, tiled=True)]
    reduce_scatter x2, waiting for transfers between devices: 29.8 us -> 0.02 us  [token_back(): lax.psum_scatter(partial_rows(jnp.int32(0), lax.axis_size('col') * row_co...]
    all_gather x1 -> x0, blocking collectives: 21.2 us -> none  [head_collect(): return lax.all_gather(values, 'row', axis=0, tiled=True)]
    unnamed x131 -> x133, local copies, waits for them, and re-layouts: 24.2 us -> 27.6 us
    unnamed x13 -> x12, waiting for transfers between devices: 48 us -> 48 us
  transfers between devices with their start and end apart: 12 -> 15, of which waited for: 10 -> 11; matrix products, arithmetic and copies ran while one was open for 20% -> 21% of each run, Pallas kernels for 0% -> 0%
where the time goes in v1:
time: 1200 us; the launch traced here: 1190 us
  waiting for transfers between devices  577 us (48%)
  local copies, waits for them, and re-layouts  222 us (18%)
  other arithmetic  174 us (14%)
  blocking collectives  142 us (12%)
  matrix products  52.1 us (4%)
  between operations  15.1 us (1%)
    reduce_scatter x2, waiting for transfers between devices, width_sums(): lax.psum_scatter(partial_rows(jnp.int32(0), lax.axis_size('row') * row_co...  173 us
    all_gather x2, waiting for transfers between devices, gradient_collect(): return lax.all_gather(values, 'row', axis=0, tiled=True)  126 us
    scatter-add x1, other arithmetic, local(): jax.ops.segment_sum(bias_grad.transpose(1, 2, 0).reshape(-1, head_local),...  113 us
    ppermute x4, waiting for transfers between devices, gather_by_bits(): lax.ppermute(line, axis, [(d, (d - have) % ways) for d in range(ways)])  101 us
    reduce_scatter x1, waiting for transfers between devices, width_back(): lax.psum_scatter(partial_rows(jnp.int32(0), lax.axis_size('row') * row_co...  94.9 us
    gather x2, local copies, waits for them, and re-layouts, local(): jnp.take(position_table, offset_index, axis=0).transpose(2, 0, 1)  51.1 us
    unnamed x12, waiting for transfers between devices  48 us
    psum x4, blocking collectives, norm_totals(): return lax.psum((jnp.sum(first_term, -1), jnp.sum(second_term, -1)), 'row')  46.2 us
  transfers between devices with their start and end apart: 15, of which 11 were waited for; matrix products, arithmetic and copies ran while one was open for 21% of the time, Pallas kernels for 0%

profile of v1, /device:TPU:0, one launch (start us, length us, event | category | flops | bytes accessed | tf_op | source)
XLA Modules:
  0.0 1192.7 jit_solution(622109002659441809)
XLA Ops:
  9.7 13.7 %all-reduce.4 = (f32[576]{0:T(1024)S(1)}, f32[576]{0:T(1024)S(1)}) all-reduce(f32[576]{0:T(1024)S(1)} %get-tuple-element.101, f32[576]{0:T(1024)S(1)} %get-tuple-element.100), channel_id=1, replica_groups=mesh['dp'=2,'row'=4,'col'=4] {'row'}, use_global_device_ids=true, to_apply=%region_3.4 | all-reduce | flops 1152 | bytes 9216 | tf_op jit(solution)/shard_map/psum | solution.py:83
  23.8 9.7 all-gather
  40.2 39.4 %gather_fusion = f32[20736,6]{1,0:T(8,128)} fusion(f32[529,6]{1,0:T(8,128)S(1)} %copy.282, s32[21504]{0:T(1024)S(1)} %pad_clamp_fusion), kind=kCustom, calls=%fused_computation | custom fusion | bytes 1078272 | tf_op jit(solution)/shard_map/jit(_take)/gather | solution.py:218
  79.7 11.6 copy.283
  93.3 47.2 %reduce-scatter.19.cloned.1.call-done = f32[576,576]{1,0:T(8,128)} async-done(((f32[2304,576]{1,0:T(8,128)}), f32[576,576]{1,0:T(8,128)}) %reduce-scatter.19.cloned.1.call-update) | async-done | bytes 1327120 | tf_op jit(solution)/shard_map/reduce_scatter | solution.py:124
  214.7 5.4 collective-permute-done
  223.1 18.8 %collective-permute-done.1 = bf16[1152,192]{0,1:T(8,128)(2,1)S(1)} collective-permute-done((bf16[1152,192]{0,1:T(8,128)(2,1)S(1)}, bf16[1152,192]{0,1:T(8,128)(2,1)S(1)}, u32[]{:S(2)}, u32[]{:S(2)}) %collective-permute-start.1) | collective-permute-done | bytes 442400 | tf_op jit(solution)/shard_map/ppermute | solution.py:22
  249.8 9.5 all-gather.2
  263.2 4.1 fusion.51
  267.4 14.9 %reduce-scatter.25.cloned.1.call-done = f32[576,192]{1,0:T(8,128)} async-done(((f32[2304,192]{1,0:T(8,128)}), f32[576,192]{1,0:T(8,128)}) %reduce-scatter.25.cloned.1.call-update) | async-done | bytes 442384 | tf_op jit(solution)/shard_map/reduce_scatter | solution.py:137
  283.7 12.0 %all-reduce.3 = (f32[576]{0:T(1024)S(1)}, f32[576]{0:T(1024)S(1)}) all-reduce(f32[576]{0:T(1024)S(1)} %get-tuple-element.99, f32[576]{0:T(1024)S(1)} %get-tuple-element.98), channel_id=1, replica_groups=mesh['dp'=2,'row'=4,'col'=4] {'row'}, use_global_device_ids=true, to_apply=%region_11.12 | all-reduce | flops 1152 | bytes 9216 | tf_op jit(solution)/shard_map/psum | solution.py:83
  296.8 8.7 all-gather.1
  309.3 4.1 fusion.50
  313.5 94.9 %reduce-scatter.23.cloned.1.call-done = f32[576,768]{1,0:T(8,128)} async-done(((f32[2304,768]{1,0:T(8,128)}), f32[576,768]{1,0:T(8,128)}) %reduce-scatter.23.cloned.1.call-update) | async-done | bytes 1769488 | tf_op jit(solution)/shard_map/reduce_scatter | solution.py:150
  408.4 126.1 %reduce-scatter.21.cloned.1.call-done = f32[576,768]{1,0:T(8,128)} async-done(((f32[2304,768]{1,0:T(8,128)}), f32[576,768]{1,0:T(8,128)}) %reduce-scatter.21.cloned.1.call-update) | async-done | bytes 1769488 | tf_op jit(solution)/shard_map/reduce_scatter | solution.py:124
  534.6 6.8 add_convert_fusion.1
  547.9 77.7 %all-gather.7.cloned.1.call-done = bf16[2304,768]{1,0:T(8,128)(2,1)} async-done(((bf16[576,768]{1,0:T(8,128)(2,1)}), bf16[2304,768]{1,0:T(8,128)(2,1)}) %all-gather.7.cloned.1.call-update) | async-done | bytes 3538960 | tf_op jit(solution)/shard_map/all_gather | solution.py:116
  625.7 4.5 fusion.52
  634.5 76.5 %collective-permute-done.3 = bf16[1152,768]{1,0:T(8,128)(2,1)S(1)} collective-permute-done((bf16[1152,768]{1,0:T(8,128)(2,1)S(1)}, bf16[1152,768]{1,0:T(8,128)(2,1)S(1)}, u32[]{:S(2)}, u32[]{:S(2)}) %collective-permute-start.3) | collective-permute-done | bytes 1769504 | tf_op jit(solution)/shard_map/ppermute | solution.py:22
  716.9 4.5 fusion.3
  724.1 11.3 all-reduce.2
  736.1 18.9 %reduce-scatter.27.cloned.1.call-done = f32[576,192]{1,0:T(8,128)} async-done(((f32[2304,192]{1,0:T(8,128)}), f32[576,192]{1,0:T(8,128)}) %reduce-scatter.27.cloned.1.call-update) | async-done | bytes 442384 | tf_op jit(solution)/shard_map/reduce_scatter | solution.py:137
  757.7 9.3 all-gather.3
  773.7 47.8 %reduce-scatter.31.cloned.1.call-done = f32[576,192]{1,0:T(8,128)} async-done(((f32[2304,192]{1,0:T(8,128)}), f32[576,192]{1,0:T(8,128)}) %reduce-scatter.31.cloned.1.call-update) | async-done | bytes 442384
  908.7 4.4 fusion.55
  914.4 47.9 %all-gather.9.cloned.1.call-done = bf16[2304,576]{1,0:T(8,128)(2,1)} async-done(((bf16[576,576]{1,0:T(8,128)(2,1)}), bf16[2304,576]{1,0:T(8,128)(2,1)}) %all-gather.9.cloned.1.call-update) | async-done | bytes 2654224 | tf_op jit(solution)/shard_map/all_gather | solution.py:116
  981.6 11.3 copy.338
  992.9 113.3 %scatter_custom_fusion = f32[529,6]{1,0:T(8,128)} fusion(s32[20736]{0:T(1024)} %reshape.280, f32[20736,6]{1,0:T(8,128)} %bitcast.150, f32[]{:T(128)} %constant.51.clone.1), kind=kCustom, calls=%fused_computation.104 | custom fusion | flops 124416 | bytes 13208 | tf_op jit(solution)/shard_map/scatter-add | solution.py:309
  1106.3 40.5 %psum.159 = f32[529,6]{1,0:T(8,128)S(1)} all-reduce(f32[529,6]{1,0:T(8,128)} %scatter_custom_fusion), channel_id=1, replica_groups=mesh['dp'=2,'row'=4,'col'=4] {'dp','row'}, use_global_device_ids=true, to_apply=%region_37.38 | all-reduce | flops 3174 | bytes 25392 | tf_op jit(solution)/shard_map/psum | solution.py:350
  1148.1 5.7 all-reduce.5
  1160.1 9.1 all-reduce.1
  1172.1 12.4 %all-reduce = (f32[192]{0:T(256)}, f32[192]{0:T(256)}, f32[192]{0:T(256)}, f32[192]{0:T(256)}) all-reduce(f32[192]{0:T(256)S(1)} %get-tuple-element.92, f32[192]{0:T(256)S(1)} %get-tuple-element.97, f32[192]{0:T(256)S(1)} %copy-done.51, f32[192]{0:T(256)S(1)} %copy-done.52), channel_id=1, replica_groups=mesh['dp'=2,'row'=4,'col'=4] {'dp','col'}, use_global_device_ids=true, to_apply=%region_29.30 | all-reduce | flops 768 | bytes 6144 | tf_op jit(solution)/shard_map/psum | solution.py:347
  (321 shorter events, 255.1 us)
Async XLA Ops:
  7.2 302.1 %copy-start = (bf16[192,768]{1,0:T(8,128)(2,1)S(1)}, bf16[192,768]{1,0:T(8,128)(2,1)}, u32[]{:S(2)}) copy-start(bf16[192,768]{1,0:T(8,128)(2,1)} %param.32) | copy-start | bytes 884740
  7.2 16.2 %copy-start.47 = (f32[192]{0:T(256)S(1)}, f32[192]{0:T(256)}, u32[]{:S(2)}) copy-start(f32[192]{0:T(256)} %param.23) | copy-start | bytes 2308
  7.2 16.2 %copy-start.54 = (f32[192]{0:T(256)S(1)}, f32[192]{0:T(256)}, u32[]{:S(2)}) copy-start(f32[192]{0:T(256)} %param.24) | copy-start | bytes 2308
  7.2 133.3 %reduce-scatter.19.cloned.1.call-start = ((), (), s32[]{:S(2)}) async-start(), calls=%async_computation.8 | async-start | bytes 7372800 | tf_op jit(solution)/shard_map/reduce_scatter | solution.py:124
  9.3 25.8 %copy-start.21 = (bf16[192,576]{1,0:T(8,128)(2,1)}, bf16[192,576]{1,0:T(8,128)(2,1)S(1)}, u32[]{:S(2)}) copy-start(bf16[192,576]{1,0:T(8,128)(2,1)S(1)} %reshape_reshape.6) | copy-start | bytes 663556
  9.4 272.9 %copy-start.4 = (f32[576,192]{1,0:T(8,128)}, f32[576,192]{1,0:T(8,128)S(1)}, u32[]{:S(2)}) copy-start(f32[576,192]{1,0:T(8,128)S(1)} %reshape.268) | copy-start | bytes 1327108
  38.7 243.6 %reduce-scatter.25.cloned.1.call-start = ((), (), s32[]{:S(2)}) async-start(), calls=%async_computation.13 | async-start | bytes 2949120 | tf_op jit(solution)/shard_map/reduce_scatter | solution.py:137
  209.5 13.5 %copy-start.42 = (bf16[96,1,384]{2,0,1:T(8,128)(2,1)S(1)}, bf16[96,1,384]{2,0,1:T(8,128)(2,1)}, u32[]{:S(2)}) copy-start(bf16[96,1,384]{2,0,1:T(8,128)(2,1)} %param.28) | copy-start | bytes 221188
  212.1 8.1 collective-permute-start
  220.3 21.7 %collective-permute-start.1 = (bf16[1152,192]{0,1:T(8,128)(2,1)S(1)}, bf16[1152,192]{0,1:T(8,128)(2,1)S(1)}, u32[]{:S(2)}, u32[]{:S(2)}) collective-permute-start(bf16[1152,192]{0,1:T(8,128)(2,1)S(1)} %pad_maximum_fusion.14), channel_id=1, source_target_pairs={{0,8},{4,12},{8,0},{12,4},{1,9},{5,13},{9,1},{13,5},{2,10},{6,14},... | collective-permute-start | bytes 1327112 | tf_op jit(solution)/shard_map/ppermute | solution.py:22
  223.1 21.2 %copy-start.31 = (bf16[192,192]{1,0:T(8,128)(2,1)}, bf16[192,192]{1,0:T(8,128)(2,1)S(1)}, u32[]{:S(2)}) copy-start(bf16[192,192]{1,0:T(8,128)(2,1)S(1)} %reshape.250) | copy-start | bytes 221188
  248.1 160.3 %reduce-scatter.23.cloned.1.call-start = ((), (), s32[]{:S(2)}) async-start(), calls=%async_computation.10 | async-start | bytes 8847360 | tf_op jit(solution)/shard_map/reduce_scatter | solution.py:150
  249.3 13.9 %copy-start.24 = (bf16[768,192]{1,0:T(8,128)(2,1)}, bf16[768,192]{1,0:T(8,128)(2,1)S(1)}, u32[]{:S(2)}) copy-start(bf16[768,192]{1,0:T(8,128)(2,1)S(1)} %reshape.251) | copy-start | bytes 884740
  263.2 639.3 %copy-start.9 = (bf16[2304,192]{0,1:T(8,128)(2,1)}, bf16[2304,192]{0,1:T(8,128)(2,1)S(1)}, u32[]{:S(2)}) copy-start(bf16[2304,192]{0,1:T(8,128)(2,1)S(1)} %reshape.294) | copy-start | bytes 2654212
  267.3 15.0 %copy-start.55 = (f32[192]{0:T(256)S(1)}, f32[192]{0:T(256)}, u32[]{:S(2)}) copy-start(f32[192]{0:T(256)} %param.29) | copy-start | bytes 2308
  267.3 28.4 %copy-start.49 = (f32[192]{0:T(256)S(1)}, f32[192]{0:T(256)}, u32[]{:S(2)}) copy-start(f32[192]{0:T(256)} %param.30) | copy-start | bytes 2308
  267.3 267.2 %reduce-scatter.21.cloned.1.call-start = ((), (), s32[]{:S(2)}) async-start(), calls=%async_computation.9 | async-start | bytes 8847360 | tf_op jit(solution)/shard_map/reduce_scatter | solution.py:124
  313.4 221.1 %copy-start.45 = (f32[768]{0:T(1024)S(1)}, f32[768]{0:T(1024)}, u32[]{:S(2)}) copy-start(f32[768]{0:T(1024)} %param.33) | copy-start | bytes 9220
  313.4 312.3 %all-gather.7.cloned.1.call-start = ((), (), s32[]{:S(2)}) async-start(), calls=%async_computation.11 | async-start | bytes 4423680 | tf_op jit(solution)/shard_map/all_gather | solution.py:116
  541.4 180.1 %reduce-scatter.29.cloned.1.call-start = ((), (), s32[]{:S(2)}) async-start(), calls=%async_computation.15 | async-start | bytes 2949120 | tf_op jit(solution)/shard_map/reduce_scatter | solution.py:163
  545.0 85.3 %collective-permute-start.2 = (bf16[576,768]{1,0:T(8,128)(2,1)}, bf16[576,768]{1,0:T(8,128)(2,1)S(1)}, u32[]{:S(2)}, u32[]{:S(2)}) collective-permute-start(bf16[576,768]{1,0:T(8,128)(2,1)} %get-tuple-element.131), channel_id=1, source_target_pairs={{0,12},{4,0},{8,4},{12,8},{1,13},{5,1},{9,5},{13,9},{2,14},{6,2},{... | collective-permute-start | bytes 2654216 | tf_op jit(solution)/shard_map/ppermute | solution.py:22
  630.3 124.7 %reduce-scatter.27.cloned.1.call-start = ((), (), s32[]{:S(2)}) async-start(), calls=%async_computation.14 | async-start | bytes 2949120 | tf_op jit(solution)/shard_map/reduce_scatter | solution.py:137
  631.6 79.5 %collective-permute-start.3 = (bf16[1152,768]{1,0:T(8,128)(2,1)S(1)}, bf16[1152,768]{1,0:T(8,128)(2,1)S(1)}, u32[]{:S(2)}, u32[]{:S(2)}) collective-permute-start(bf16[1152,768]{1,0:T(8,128)(2,1)S(1)} %pad_maximum_fusion), channel_id=1, source_target_pairs={{0,8},{4,12},{8,0},{12,4},{1,9},{5,13},{9,1},{13,5},{2,10},{6,14},... | collective-permute-start | bytes 5308424 | tf_op jit(solution)/shard_map/ppermute | solution.py:22
  721.4 33.6 %copy-start.13 = (f32[576,192]{1,0:T(8,128)S(1)}, f32[576,192]{1,0:T(8,128)}, u32[]{:S(2)}) copy-start(f32[576,192]{1,0:T(8,128)} %copy-done.12) | copy-start | bytes 1327108
  721.4 100.1 %reduce-scatter.31.cloned.1.call-start = ((), (), s32[]{:S(2)}) async-start(), calls=%async_computation.16 | async-start | bytes 2949120
  770.9 142.2 %copy-start.6 = (bf16[2304,192]{0,1:T(8,128)(2,1)}, bf16[2304,192]{0,1:T(8,128)(2,1)S(1)}, u32[]{:S(2)}) copy-start(bf16[2304,192]{0,1:T(8,128)(2,1)S(1)} %reshape.296) | copy-start | bytes 2654212
  772.9 189.4 %all-gather.9.cloned.1.call-start = ((), (), s32[]{:S(2)}) async-start(), calls=%async_computation.12 | async-start | bytes 3686400 | tf_op jit(solution)/shard_map/all_gather | solution.py:116
  902.4 251.5 %all-reduce.9.cloned.1.call-start = ((), (), s32[]{:S(2)}) async-start(), calls=%async_computation.18 | async-start | bytes 3538944 | tf_op jit(solution)/shard_map/psum | solution.py:334
  971.0 187.6 %reduce-scatter.33.cloned.1.call-start = ((), (), s32[]{:S(2)}) async-start(), calls=%async_computation.17 | async-start | bytes 2949120 | tf_op jit(solution)/shard_map/reduce_scatter | solution.py:163
  1148.1 21.1 %copy-start.20 = (f32[576,192]{1,0:T(8,128)S(1)}, f32[576,192]{1,0:T(8,128)}, u32[]{:S(2)}) copy-start(f32[576,192]{1,0:T(8,128)} %get-tuple-element.127) | copy-start | bytes 1327108
  1160.1 24.3 %copy-start.39 = (f32[96,1,384]{2,1,0:T(1,128)S(1)}, f32[96,1,384]{2,1,0:T(1,128)}, u32[]{:S(2)}) copy-start(f32[96,1,384]{2,1,0:T(1,128)} %get-tuple-element.155) | copy-start | bytes 442372
  1169.2 15.9 %copy-start.33 = (f32[192,768]{1,0:T(8,128)S(1)}, f32[192,768]{1,0:T(8,128)}, u32[]{:S(2)}) copy-start(f32[192,768]{1,0:T(8,128)} %get-tuple-element.159) | copy-start | bytes 1769476
  (46 other events, 149.3 us)
Sparse Core Ops, SparseCore 0:
  38.8 101.6 reduce-scatter.18
  248.2 34.0 reduce-scatter.24
  284.7 123.6 reduce-scatter.22
  410.7 123.8 reduce-scatter.20
  541.5 84.1 all-gather.6
  630.4 34.1 reduce-scatter.28
  721.5 33.4 reduce-scatter.26
  773.1 48.4 reduce-scatter.30
  902.5 59.7 all-gather.8
  971.1 54.9 all-reduce.8
  1028.7 33.0 reduce-scatter.32
